TPU v7x, 128 devices: a whole 4x4x4 slice. The times are simulated.
128 devices in a mesh: sec: 2 (over core), dev: 64 (over z, x, y).
Axes of the slice: x: 4, y: 4, z: 4, core: 2. Of those that a mesh axis runs over, the one named last changes fastest.
Arguments:
- hidden_in: bfloat16 [2, 16, 4096], P('sec'), may hold values from -0.3125 to 0.3125
- queries: bfloat16 [2, 64, 16, 128], P('sec', 'dev'), may hold values from -4 to 4
- key_cache: bfloat16 [2, 64, 4096, 128], P('sec', 'dev'), may hold values from -12 to 12
- value_cache: bfloat16 [2, 64, 4096, 128], P('sec', 'dev'), may hold values from -6 to 6
- kv_lengths: int32 [2, 16], P('sec'), may hold values from 2 to 4096, as said below
- route_ids: int32 [2, 16, 8], replicated, may hold values from 0 to 63, all different within a row; in each aligned block of 16 rows (0 to 15, 16 to 31, ..., all dimensions but the last counted through in order) at most 4 rows name the same one
- out_weight: bfloat16 [8192, 4096], P('dev'), may hold values from -0.0625 to 0.0625
- norm_gain: bfloat16 [4096], replicated, may hold values from 0.099609375 to 1.8984375
- router_weight: bfloat16 [4096, 64], replicated, may hold values from -0.1875 to 0.1875
- w_gate: bfloat16 [64, 4096, 1536], P('dev', None, 'sec'), may hold values from -0.09375 to 0.09375
- w_up: bfloat16 [64, 4096, 1536], P('dev', None, 'sec'), may hold values from -0.09375 to 0.09375
- w_down: bfloat16 [64, 1536, 4096], P('dev', 'sec'), may hold values from -0.15625 to 0.15625
Outputs:
- mixed: bfloat16 [2, 16, 4096], P('sec', None, 'dev')
Inputs may be any that keep to these rules, and one draw needn't show every extreme that they name: `route_ids`: no expert is chosen by more than 4 tokens of one micro-batch, and in some micro-batch some expert is chosen by exactly 4. `kv_lengths`: some sequence uses all 4096 positions.
All inputs are finite; a program needn't handle non-finite values.
Results may differ from a plain program's by a relative error of at most 0.018.
Values may be sent and summed in bfloat16 or wider, within the bound.
A program may use at most 128 MiB of HBM per device.

v0:
```python
import jax
import jax.numpy as jnp
from jax import lax
from jax.sharding import PartitionSpec as P

MASKED_SCORE = -1e30
NORM_EPS = 1e-06


def swapped(value, axis, bit):
    mask = 2**bit
    pairs = [(source, source ^ mask) for source in range(lax.axis_size(axis))]
    return lax.ppermute(value, axis, pairs)


def expert_rows(tokens_in, gate_half, up_half, down_half):
    gate_proj = jnp.dot(tokens_in, gate_half, preferred_element_type=jnp.float32)
    up_proj = jnp.dot(tokens_in, up_half, preferred_element_type=jnp.float32)
    hidden = (jax.nn.silu(gate_proj) * up_proj).astype(jnp.bfloat16)
    return jnp.dot(hidden, down_half, preferred_element_type=jnp.float32)


def body(
    hidden_in,
    queries,
    key_cache,
    value_cache,
    kv_lengths,
    route_ids,
    out_weight,
    norm_gain,
    router_weight,
    w_gate,
    w_up,
    w_down,
):
    piece_count = queries.shape[1]
    group_size = queries.shape[2]
    head_dim = queries.shape[3]
    kv_span = key_cache.shape[2]
    seq_count = hidden_in.shape[1]
    model_width = hidden_in.shape[2]
    devices = lax.axis_size("dev")
    my_rank = lax.axis_index("dev")
    sec_index = lax.axis_index("sec")
    kv_count = piece_count * devices // seq_count
    head_count = kv_count * group_size
    per_device = head_count // devices
    scores = jnp.einsum(
        "pgh,plh->pgl", queries[0], key_cache[0], preferred_element_type=jnp.float32
    ) * head_dim ** (-0.5)
    piece_ids = my_rank * piece_count + jnp.arange(piece_count, dtype=jnp.int32)
    lengths = jnp.take(kv_lengths[0], piece_ids // kv_count)
    is_valid = (jnp.arange(kv_span, dtype=jnp.int32)[None, :] < lengths[:, None])[:, None, :]
    scores = jnp.where(is_valid, scores, MASKED_SCORE)
    local_max = jnp.max(scores, axis=-1, keepdims=True)
    weights = jnp.where(is_valid, jnp.exp(scores - local_max), 0.0)
    local_sum = jnp.sum(weights, axis=-1, keepdims=True)
    local_out = jnp.einsum(
        "pgl,plh->pgh", weights, value_cache[0].astype(jnp.float32), precision=lax.Precision.HIGHEST
    )
    attended = (local_out / local_sum).astype(jnp.bfloat16)
    everything = lax.all_gather(attended, "dev", axis=0, tiled=True)
    everything = everything.reshape(seq_count, head_count, head_dim)
    mine = lax.dynamic_slice_in_dim(everything, my_rank * per_device, per_device, 1)
    projected = jnp.dot(
        mine.reshape(seq_count, per_device * head_dim),
        out_weight,
        preferred_element_type=jnp.float32,
    )
    residual = hidden_in[0].astype(jnp.float32) + lax.psum(projected, "dev")
    normed = (
        residual
        * lax.rsqrt(jnp.mean(residual * residual, axis=-1, keepdims=True) + NORM_EPS)
        * norm_gain.astype(jnp.float32)
    ).astype(jnp.bfloat16)
    expert_total = router_weight.shape[1]
    local_experts = w_gate.shape[0]
    logits = jnp.dot(normed, router_weight, preferred_element_type=jnp.float32)
    own_routes = lax.dynamic_index_in_dim(route_ids, sec_index, 0, keepdims=False)
    onehot = own_routes[:, :, None] == jnp.arange(expert_total, dtype=jnp.int32)[None, None, :]
    picked = jnp.sum(jnp.where(onehot, logits[:, None, :], 0.0), axis=-1)
    sig_scores = jax.nn.sigmoid(picked)
    gate_share = sig_scores / jnp.sum(sig_scores, axis=-1, keepdims=True)
    expert_ids = my_rank * local_experts + jnp.arange(local_experts, dtype=jnp.int32)
    matches = own_routes[None, :, :] == expert_ids[:, None, None]
    own_share = jnp.sum(jnp.where(matches, gate_share[None], 0.0), axis=-1)
    is_first = sec_index == 0
    partner_rows, partner_share = (
        swapped(normed, "sec", 0),
        swapped(own_share.astype(jnp.bfloat16), "sec", 0).astype(own_share.dtype),
    )
    rows_both = jnp.where(
        is_first,
        jnp.concatenate([normed, partner_rows], axis=0),
        jnp.concatenate([partner_rows, normed], axis=0),
    )
    share_both = jnp.where(
        is_first,
        jnp.concatenate([own_share, partner_share], axis=1),
        jnp.concatenate([partner_share, own_share], axis=1),
    )
    expert_out = expert_rows(rows_both, w_gate[0], w_up[0], w_down[0])
    routed_sum = expert_out * share_both[0][:, None]
    routed_sum = routed_sum.reshape(2, seq_count, model_width)
    col_width = model_width // devices
    by_batch = lax.psum_scatter(
        routed_sum.astype(jnp.bfloat16), "sec", scatter_dimension=0, tiled=True
    ).astype(jnp.float32)
    my_block = lax.psum_scatter(by_batch, "dev", scatter_dimension=2, tiled=True)[0]
    residual_part = lax.dynamic_slice_in_dim(residual, my_rank * col_width, col_width, 1)
    return (residual_part + my_block).astype(jnp.bfloat16)[None]


def solution(mesh):
    placed = (
        P("sec", None, None),
        P("sec", "dev", None, None),
        P("sec", "dev", None, None),
        P("sec", "dev", None, None),
        P("sec", None),
        P(),
        P("dev", None),
        P(),
        P(),
        P("dev", None, "sec"),
        P("dev", None, "sec"),
        P("dev", "sec", None),
    )
    return jax.shard_map(
        body, mesh=mesh, in_specs=placed, out_specs=P("sec", None, "dev"), check_vma=False
    )
```

profile of v0, /device:TPU:0, one launch (start us, length us, event | category | flops | bytes accessed | tf_op | source)
XLA Modules:
  0.0 703.6 jit_solution(14132858356391595830)
XLA Ops:
  6.5 1.4 fusion.37
  7.9 0.6 iota_compare_fusion.1
  8.5 1.2 fusion.38
  9.7 0.2 fusion.16
  10.0 1.8 fusion.13
  11.8 179.4 %all-gather = bf16[1024,128]{1,0:T(8,128)(2,1)S(1)} all-gather(bf16[16,128]{1,0:T(8,128)(2,1)S(1)} %fusion.13), channel_id=2, replica_groups=mesh['sec'=2,'dev'=64] {'dev'}, dimensions={0}, use_global_device_ids=true | all-gather | bytes 266240 | tf_op jit(solution)/shard_map/all_gather | solution.py:63
  191.2 2.2 fusion.27
  193.4 0.0 all-reduce.2.cloned.1.call-update
  193.4 0.0 reduce-scatter.5.cloned.1.call-start
  193.5 0.7 dynamic-slice_bitcast_fusion
  194.1 0.1 copy.22
  194.2 0.7 convert_element_type.53
  194.9 117.3 %all-reduce.2.cloned.1.call-done = f32[16,4096]{1,0:T(8,128)} async-done(((f32[16,4096]{1,0:T(8,128)}), f32[16,4096]{1,0:T(8,128)}) %all-reduce.2.cloned.1.call-update) | async-done | bytes 262160 | tf_op jit(solution)/shard_map/psum | solution.py:71
  312.3 1.1 multiply_reduce_fusion
  313.4 0.1 multiply_convert_fusion
  313.5 0.1 collective-permute-start
  313.6 1.3 fusion.39
  314.9 0.2 select_reduce_fusion
  315.1 0.1 copy.23
  315.2 0.6 collective-permute-start.1
  315.8 0.8 collective-permute-done.1
  316.6 0.1 broadcast_select_fusion
  316.7 4.0 fusion.2
  320.6 7.9 %fusion.9 = bf16[32,4096]{1,0:T(8,128)(2,1)} fusion(bf16[1,768,4096]{2,1,0:T(8,128)(2,1)} %param.23, f32[32]{0:T(128)S(1)} %broadcast_select_fusion, f32[32,768]{1,0:T(8,128)S(1)} %fusion.2, bf16[1,4096,768]{2,1,0:T(8,128)(2,1)} %param.21, bf16[16,4096]{1,0:T(8,128)(2,1)S(1)} %collective-permute-done, bf16[16,4096]{1,0:T(8,128)(2,1)S(1)} %multiply_convert_fusion, ...), kind=kOutput, calls=%fused_computation.7 | convolution fusion | flops 404242432 | bytes 13205633 | tf_op jit(solution)/shard_map/dot_general | solution.py:20
  328.6 0.0 reduce-scatter.5.cloned.1.call-update
  328.6 0.0 reduce-scatter.7.cloned.1.call-start
  328.6 7.7 %reduce-scatter.5.cloned.1.call-done = bf16[1,16,4096]{2,1,0:T(8,128)(2,1)} async-done(((bf16[2,16,4096]{2,1,0:T(8,128)(2,1)}), bf16[1,16,4096]{2,1,0:T(8,128)(2,1)}) %reduce-scatter.5.cloned.1.call-update) | async-done | bytes 131088 | tf_op jit(solution)/shard_map/reduce_scatter | solution.py:107
  336.3 4.7 copy.24
  341.0 0.0 reduce-scatter.7.cloned.1.call-update
  341.0 354.5 %reduce-scatter.7.cloned.1.call-done = f32[64,16]{1,0:T(8,128)} async-done(((f32[4096,16]{1,0:T(8,128)}), f32[64,16]{1,0:T(8,128)}) %reduce-scatter.7.cloned.1.call-update) | async-done | bytes 4112
  695.6 0.8 copy.25
  696.4 0.7 fusion.26
  (12 shorter events, 0.1 us)
Async XLA Ops:
  6.5 2.0 copy-start
  6.5 308.6 %copy-start.1 = (s32[2,16,8]{1,2,0:T(8,128)S(1)}, s32[2,16,8]{1,2,0:T(8,128)}, u32[]{:S(2)}) copy-start(s32[2,16,8]{1,2,0:T(8,128)} %param.17) | copy-start | bytes 3076
  6.5 305.7 %all-reduce.2.cloned.1.call-start = ((), (), s32[]{:S(2)}) async-start(), calls=%async_computation.2 | async-start | bytes 524288 | tf_op jit(solution)/shard_map/psum | solution.py:71
  193.4 142.9 %reduce-scatter.5.cloned.1.call-start = ((), (), s32[]{:S(2)}) async-start(), calls=%async_computation.3 | async-start | bytes 393216 | tf_op jit(solution)/shard_map/reduce_scatter | solution.py:107
  313.5 3.2 collective-permute-start
  315.2 1.4 collective-permute-start.1
  328.6 367.0 %reduce-scatter.7.cloned.1.call-start = ((), (), s32[]{:S(2)}) async-start(), calls=%async_computation.4 | async-start | bytes 2129920
Sparse Core Ops, SparseCore 0:
  193.5 118.6 all-reduce.1
  328.7 7.5 reduce-scatter.4
  341.1 354.3 reduce-scatter.6
where the time goes:
time: 704 us
  waiting for transfers between devices  480 us (68%)
  blocking collectives  179 us (25%)
  matrix products  18.3 us (3%)
  between operations  13.2 us (2%)
    unnamed x4, waiting for transfers between devices  355 us
    all_gather x1, blocking collectives, body(): everything = lax.all_gather(attended, 'dev', axis=0, tiled=True)  179 us
    psum x1, waiting for transfers between devices, body(): residual = hidden_in[0].astype(jnp.float32) + lax.psum(projected, 'dev')  117 us
  transfers between devices with their start and end apart: 5, of which 4 were waited for; matrix products, arithmetic and copies ran while one was open for 0% of the time, Pallas kernels for 0%

commit v1 on v0

v1 whole, which is shorter than its diff:
```python
import functools

import jax
import jax.numpy as jnp
from jax import lax
from jax.experimental import pallas as pl
from jax.experimental.pallas import tpu as pltpu
from jax.sharding import PartitionSpec as P

MASKED_SCORE = -1e30
NORM_EPS = 1e-06
MESH = pl.DeviceIdType.MESH
LANES = 128
CAP = 4
SIDE = 4
PLANE = SIDE * SIDE
RING_ORDER = (2, 1, 3, 0)


def hops(step):
    return min(step, SIDE - step)


def far_first(steps):
    return sorted(steps, key=lambda step: -sum(hops(part) for part in step))


PLANE_STEPS = far_first([(dx, dy) for dx in range(SIDE) for dy in range(SIDE)])
CUBE_STEPS = far_first(
    [(dz, dx, dy) for dz in range(SIDE) for dx in range(SIDE) for dy in range(SIDE)]
)


def layer_kernel(
    hidden_ref,
    query_ref,
    key_hbm,
    value_hbm,
    length_ref,
    route_ref,
    out_weight_hbm,
    gain_ref,
    router_hbm,
    gate_hbm,
    up_hbm,
    down_hbm,
    out_ref,
    key_buf,
    value_buf,
    out_weight_buf,
    router_buf,
    gate_buf,
    up_buf,
    down_buf,
    att_out,
    att_in,
    part_out,
    part_in,
    block_out,
    rows_in,
    own_half,
    other_half,
    half_in,
    comb_out,
    comb_in,
    load_sem,
    att_send,
    att_recv,
    part_send,
    part_recv,
    rows_send,
    rows_recv,
    half_send,
    half_recv,
    comb_send,
    comb_recv,
):
    s = lax.axis_index("sec")
    d = lax.axis_index("dev")
    z = d // PLANE
    x = lax.rem(d // SIDE, SIDE)
    y = lax.rem(d, SIDE)
    seqs = hidden_ref.shape[1]
    kv_span = key_buf.shape[0]
    head_dim = key_buf.shape[1]
    width = out_weight_buf.shape[1]
    rows = 2 * seqs
    chunk = width // SIDE
    chunk_blocks = chunk // LANES

    loads = [
        pltpu.make_async_copy(src, dst, load_sem.at[i])
        for i, (src, dst) in enumerate(
            (
                (key_hbm.at[0, 0], key_buf),
                (value_hbm.at[0, 0], value_buf),
                (out_weight_hbm, out_weight_buf),
                (gate_hbm.at[0], gate_buf),
                (up_hbm.at[0], up_buf),
                (router_hbm, router_buf),
                (down_hbm.at[0], down_buf),
            )
        )
    ]
    for load in loads:
        load.start()

    zs = [lax.rem(z + i, SIDE) for i in range(SIDE)]
    xs = [lax.rem(x + i, SIDE) for i in range(SIDE)]
    ys = [lax.rem(y + i, SIDE) for i in range(SIDE)]

    def at(dz, dx, dy):
        return zs[dz] * PLANE + xs[dx] * SIDE + ys[dy]

    barrier = pltpu.get_barrier_semaphore()
    for step in CUBE_STEPS[:-1]:
        pl.semaphore_signal(barrier, inc=1, device_id=(s, at(*step)), device_id_type=MESH)
    pl.semaphore_signal(barrier, inc=1, device_id=(1 - s, d), device_id_type=MESH)

    loads[0].wait()
    scores = lax.dot_general(
        query_ref[0, 0], key_buf[...], (((1,), (1,)), ((), ())), preferred_element_type=jnp.float32
    ) * head_dim ** (-0.5)
    length = length_ref[0, d // SIDE]
    is_valid = lax.broadcasted_iota(jnp.int32, scores.shape, 1) < length
    scores = jnp.where(is_valid, scores, MASKED_SCORE)
    top = jnp.max(scores, axis=-1, keepdims=True)
    weights = jnp.where(is_valid, jnp.exp(scores - top), 0.0).astype(jnp.bfloat16)
    total = jnp.sum(weights.astype(jnp.float32), axis=-1, keepdims=True)
    loads[1].wait()
    attended = jnp.dot(weights, value_buf[...], preferred_element_type=jnp.float32) / total
    att_out[...] = attended.reshape(att_out.shape)

    pl.semaphore_wait(barrier, SIDE * PLANE)
    seq = d // SIDE
    for dx, dy in PLANE_STEPS:
        in_plane = xs[dx] * SIDE + ys[dy]
        src = att_out.at[in_plane]
        dst = att_in.at[seq]

        def send_row(src=src, dst=dst, target=y * PLANE + in_plane):
            pltpu.make_async_remote_copy(
                src, dst, att_send, att_recv, device_id=(s, target), device_id_type=MESH
            ).start()

        if (dx, dy) == (0, 0):
            pl.when(y != z)(send_row)

            @pl.when(y == z)
            def _():
                pltpu.make_async_copy(src, dst, att_recv).start()
        else:
            send_row()

    routes = jnp.concatenate([route_ref[0], route_ref[1]], axis=0)
    chosen = jnp.sum((routes == d).astype(jnp.float32), axis=1, keepdims=True)
    row_a = lax.broadcasted_iota(jnp.int32, (rows, rows), 0)
    row_b = lax.broadcasted_iota(jnp.int32, (rows, rows), 1)
    chosen_row = jnp.sum(jnp.where(row_a == row_b, chosen, 0.0), axis=0, keepdims=True)
    before = (row_a < row_b) & (row_a // seqs == row_b // seqs)
    rank_row = jnp.sum(jnp.where(before, chosen, 0.0), axis=0, keepdims=True)
    slot = lax.broadcasted_iota(jnp.int32, (2 * CAP, rows), 0)
    token = lax.broadcasted_iota(jnp.int32, (2 * CAP, rows), 1)
    slot_batch = jnp.where(slot < CAP, s, 1 - s)
    picked = (
        (token // seqs == slot_batch)
        & (rank_row == lax.rem(slot, CAP).astype(jnp.float32))
        & (chosen_row > 0.5)
    )
    pick = jnp.where(picked, 1.0, 0.0).astype(jnp.bfloat16)

    experts = router_buf.shape[1]
    own_routes = route_ref[s]
    expert_lane = lax.broadcasted_iota(jnp.int32, (seqs, experts), 1)
    match = jnp.zeros((seqs, experts), jnp.float32)
    for k in range(own_routes.shape[1]):
        match = match + (own_routes[:, k : k + 1] == expert_lane).astype(jnp.float32)
    lower = lax.broadcasted_iota(jnp.int32, (seqs, seqs), 0) > lax.broadcasted_iota(
        jnp.int32, (seqs, seqs), 1
    )
    rank = jnp.dot(
        lower.astype(jnp.bfloat16), match.astype(jnp.bfloat16), preferred_element_type=jnp.float32
    )
    slots = experts * CAP
    spread = (
        lax.broadcasted_iota(jnp.int32, (experts, slots), 1) // CAP
        == lax.broadcasted_iota(jnp.int32, (experts, slots), 0)
    ).astype(jnp.float32)
    rank_slots = jnp.dot(
        rank.astype(jnp.bfloat16), spread.astype(jnp.bfloat16), preferred_element_type=jnp.float32
    )
    slot_lane = lax.rem(lax.broadcasted_iota(jnp.int32, (seqs, slots), 1), CAP)
    in_slot = rank_slots == slot_lane.astype(jnp.float32)

    loads[2].wait()
    pltpu.make_async_copy(att_in, att_in, att_recv).wait()
    head_rows = att_in[...].reshape(seqs, head_dim).astype(jnp.bfloat16)
    for dz in range(SIDE):
        base = pl.multiple_of(dz * chunk, chunk)
        partial = jnp.dot(
            head_rows, out_weight_buf[:, pl.ds(base, chunk)], preferred_element_type=jnp.float32
        ).astype(jnp.bfloat16)
        for j in range(chunk_blocks):
            part_out[dz * chunk_blocks + j] = partial[:, j * LANES : (j + 1) * LANES]
    for step in CUBE_STEPS:
        target = at(*step)
        src = part_out.at[target // 2]
        dst = part_in.at[d]
        if step == (0, 0, 0):
            pltpu.make_async_copy(src, dst, part_recv).start()
        else:
            pltpu.make_async_remote_copy(
                src, dst, part_send, part_recv, device_id=(s, target), device_id_type=MESH
            ).start()

    my_block = d // 2
    my_half = lax.rem(d, 2)
    lanes_at = pl.multiple_of(my_block * LANES, LANES)
    hidden_block = hidden_ref[0, :, pl.ds(lanes_at, LANES)].astype(jnp.float32)
    gain = gain_ref[...].astype(jnp.float32)
    gain_block = gain_ref[:, pl.ds(lanes_at, LANES)].astype(jnp.float32)

    pltpu.make_async_copy(part_in, part_in, part_recv).wait()
    residual = hidden_block
    for i in range(part_in.shape[0]):
        residual = residual + part_in[i].astype(jnp.float32)
    block_out[...] = (residual * gain_block).astype(jnp.bfloat16)

    for step in CUBE_STEPS:
        dst = rows_in.at[my_block, s]

        def send_block(dst=dst, target=at(*step), dz=step[0]):
            pltpu.make_async_remote_copy(
                block_out,
                dst,
                rows_send,
                rows_recv.at[dz],
                device_id=(my_half, target),
                device_id_type=MESH,
            ).start()

        if step == (0, 0, 0):
            pl.when(my_half != s)(send_block)

            @pl.when(my_half == s)
            def _():
                pltpu.make_async_copy(block_out, dst, rows_recv.at[0]).start()
        else:
            send_block()

    inverse_square = 1.0 / (gain * gain)
    gate_proj = jnp.zeros((rows, gate_buf.shape[1]), jnp.float32)
    up_proj = jnp.zeros((rows, gate_buf.shape[1]), jnp.float32)
    squares = jnp.zeros((rows, LANES), jnp.float32)
    loads[3].wait()
    loads[4].wait()
    for dz in (0, 1, 3, 2):
        plane = lax.rem(z + SIDE - dz, SIDE)
        arrived = rows_in.at[pl.ds(plane * chunk_blocks, chunk_blocks)]
        pltpu.make_async_copy(arrived, arrived, rows_recv.at[dz]).wait()
        tokens = jnp.concatenate(
            [rows_in[plane * chunk_blocks + j].reshape(rows, LANES) for j in range(chunk_blocks)],
            axis=1,
        )
        base = pl.multiple_of(plane * chunk, chunk)
        gate_proj = gate_proj + jnp.dot(
            tokens, gate_buf[pl.ds(base, chunk), :], preferred_element_type=jnp.float32
        )
        up_proj = up_proj + jnp.dot(
            tokens, up_buf[pl.ds(base, chunk), :], preferred_element_type=jnp.float32
        )
        wide = tokens.astype(jnp.float32)
        gain_part = gain_ref[:, pl.ds(base, chunk)].astype(jnp.float32)
        wide = wide * wide * (1.0 / (gain_part * gain_part))
        for j in range(chunk_blocks):
            squares = squares + wide[:, j * LANES : (j + 1) * LANES]
    scale = lax.rsqrt(jnp.sum(squares, axis=1, keepdims=True) / width + NORM_EPS)
    gate_proj = gate_proj * scale
    up_proj = up_proj * scale
    hidden = (gate_proj * jax.nn.sigmoid(gate_proj) * up_proj).astype(jnp.bfloat16)
    packed = jnp.dot(pick, hidden, preferred_element_type=jnp.float32).astype(jnp.bfloat16)

    loads[6].wait()

    def half_copy(order):
        plane = zs[RING_ORDER[order]]
        where = pl.ds(plane * chunk_blocks, chunk_blocks)
        return pltpu.make_async_remote_copy(
            other_half.at[where],
            half_in.at[where],
            half_send.at[order],
            half_recv.at[order],
            device_id=(1 - s, d),
            device_id_type=MESH,
        )

    def down(order):
        plane = zs[RING_ORDER[order]]
        base = pl.multiple_of(plane * chunk, chunk)
        product = jnp.dot(packed, down_buf[:, pl.ds(base, chunk)], preferred_element_type=jnp.float32)
        for j in range(chunk_blocks):
            block = product[:, j * LANES : (j + 1) * LANES]
            own_half[plane * chunk_blocks + j] = block[:CAP]
            other_half[plane * chunk_blocks + j] = block[CAP:]
        half_copy(order).start()

    def combine(order):
        dz = RING_ORDER[order]
        where = pl.ds(zs[dz] * chunk_blocks, chunk_blocks)
        half_copy(order).wait_recv()
        comb_out[where] = own_half[where] + half_in[where]
        for dx, dy in PLANE_STEPS:
            target = at(dz, dx, dy)
            src = comb_out.at[target // 2]
            dst = comb_in.at[d]
            if (dz, dx, dy) == (0, 0, 0):
                pltpu.make_async_copy(src, dst, comb_recv).start()
            else:
                pltpu.make_async_remote_copy(
                    src, dst, comb_send, comb_recv, device_id=(s, target), device_id_type=MESH
                ).start()

    down(0)
    for order in range(1, SIDE):
        down(order)
        combine(order - 1)
    combine(SIDE - 1)

    loads[5].wait()
    logits = jnp.zeros((seqs, experts), jnp.float32)
    own_tokens = jnp.concatenate([rows_in[k, s] for k in range(rows_in.shape[0])], axis=1)
    logits = jnp.dot(own_tokens, router_buf[...], preferred_element_type=jnp.float32)
    own_scale = jnp.where(s == 0, scale[:seqs], scale[seqs:])
    shares = match * jax.nn.sigmoid(logits * own_scale)
    gates = shares / jnp.sum(shares, axis=1, keepdims=True)
    gate_slots = jnp.where(
        in_slot,
        jnp.dot(
            gates, spread, precision=lax.Precision.HIGHEST, preferred_element_type=jnp.float32
        ),
        0.0,
    )

    pltpu.make_async_copy(comb_in, comb_in, comb_recv).wait()
    routed = jnp.dot(
        gate_slots,
        comb_in[...].reshape(slots, LANES),
        precision=lax.Precision.HIGHEST,
        preferred_element_type=jnp.float32,
    )
    mixed = residual + routed
    features = out_ref.shape[2]
    out_ref[0] = jnp.where(my_half == 0, mixed[:, :features], mixed[:, features:]).astype(
        out_ref.dtype
    )

    for order in range(SIDE):
        half_copy(order).wait_send()
    most = att_in.at[pl.ds(0, PLANE - 1)]
    pltpu.make_async_copy(most, most, att_send).wait()

    @pl.when(y != z)
    def _():
        pltpu.make_async_copy(att_in.at[0], att_in.at[0], att_send).wait()

    most = part_in.at[pl.ds(0, SIDE * PLANE - 1)]
    pltpu.make_async_copy(most, most, part_send).wait()
    pltpu.make_async_copy(most, most, rows_send).wait()

    @pl.when(my_half != s)
    def _():
        pltpu.make_async_copy(block_out, block_out, rows_send).wait()

    most = comb_in.at[pl.ds(0, SIDE * PLANE - 1)]
    pltpu.make_async_copy(most, most, comb_send).wait()


def body(
    hidden_in,
    queries,
    key_cache,
    value_cache,
    kv_lengths,
    route_ids,
    out_weight,
    norm_gain,
    router_weight,
    w_gate,
    w_up,
    w_down,
):
    seqs, width = hidden_in.shape[1:]
    kv_span, head_dim = key_cache.shape[2:]
    experts = router_weight.shape[1]
    hidden_units = w_gate.shape[2]
    devices = lax.axis_size("dev")
    blocks = width // LANES
    vmem = pl.BlockSpec(memory_space=pltpu.VMEM)
    hbm = pl.BlockSpec(memory_space=pl.ANY)
    smem = pl.BlockSpec(memory_space=pltpu.SMEM)
    dma = pltpu.SemaphoreType.DMA
    return pl.pallas_call(
        layer_kernel,
        out_shape=jax.ShapeDtypeStruct((1, seqs, width // devices), jnp.bfloat16),
        in_specs=[vmem, vmem, hbm, hbm, smem, vmem, hbm, vmem, hbm, hbm, hbm, hbm],
        out_specs=vmem,
        scratch_shapes=[
            pltpu.VMEM((kv_span, head_dim), jnp.bfloat16),
            pltpu.VMEM((kv_span, head_dim), jnp.bfloat16),
            pltpu.VMEM(out_weight.shape, jnp.bfloat16),
            pltpu.VMEM(router_weight.shape, jnp.bfloat16),
            pltpu.VMEM((width, hidden_units), jnp.bfloat16),
            pltpu.VMEM((width, hidden_units), jnp.bfloat16),
            pltpu.VMEM((hidden_units, width), jnp.bfloat16),
            pltpu.VMEM((seqs, 1, head_dim), jnp.float32),
            pltpu.VMEM((seqs, 1, head_dim), jnp.float32),
            pltpu.VMEM((blocks, seqs, LANES), jnp.bfloat16),
            pltpu.VMEM((devices, seqs, LANES), jnp.bfloat16),
            pltpu.VMEM((seqs, LANES), jnp.bfloat16),
            pltpu.VMEM((blocks, 2, seqs, LANES), jnp.bfloat16),
            pltpu.VMEM((blocks, CAP, LANES), jnp.float32),
            pltpu.VMEM((blocks, CAP, LANES), jnp.float32),
            pltpu.VMEM((blocks, CAP, LANES), jnp.float32),
            pltpu.VMEM((blocks, CAP, LANES), jnp.float32),
            pltpu.VMEM((devices, CAP, LANES), jnp.float32),
            dma((7,)),
            dma,
            dma,
            dma,
            dma,
            dma,
            dma((SIDE,)),
            dma((SIDE,)),
            dma((SIDE,)),
            dma,
            dma,
        ],
        compiler_params=pltpu.CompilerParams(
            collective_id=0, has_side_effects=True, vmem_limit_bytes=56 * 2**20
        ),
    )(
        hidden_in,
        queries,
        key_cache,
        value_cache,
        kv_lengths,
        route_ids,
        out_weight,
        norm_gain.reshape(1, width),
        router_weight,
        w_gate,
        w_up,
        w_down,
    )


def solution(mesh):
    placed = (
        P("sec", None, None),
        P("sec", "dev", None, None),
        P("sec", "dev", None, None),
        P("sec", "dev", None, None),
        P("sec", None),
        P(),
        P("dev", None),
        P(),
        P(),
        P("dev", None, "sec"),
        P("dev", None, "sec"),
        P("dev", "sec", None),
    )
    return jax.shard_map(
        body, mesh=mesh, in_specs=placed, out_specs=P("sec", None, "dev"), check_vma=False
    )
```

time: 704 us -> 45.5 us (0.06)
  the two profiles are of different devices: /device:TPU:0 before, /device:TPU:1 now
where the time goes in v1:
time: 45.5 us; the launch traced here: 45.2 us
  Pallas kernels  38.9 us (85%)
  local copies, waits for them, and re-layouts  6.31 us (14%)
    pallas_call x1, Pallas kernels, body(): pl.pallas_call(layer_kernel, out_shape=jax.ShapeDtypeStruct((1, seqs, wid...  38.9 us
    unnamed x3, local copies, waits for them, and re-layouts  5.01 us
    reshape x1, local copies, waits for them, and re-layouts, body(): norm_gain.reshape(1, width)  1.3 us

profile of v1, /device:TPU:1, one launch (start us, length us, event | category | flops | bytes accessed | tf_op | source)
XLA Modules:
  0.0 45.2 jit_solution(3947936174205677443)
XLA Ops:
  0.0 1.4 %copy.13.route_ref = s32[2,16,8]{2,1,0:T(8,128)} copy(s32[2,16,8]{1,2,0:T(8,128)} %param.17) | data formatting | bytes 2048 | tf_op args[5]
  1.4 1.3 %reshape.3.gain_ref = bf16[1,4096]{1,0:T(2,128)(2,1)} reshape(bf16[4096]{0:T(1024)(128)(2,1)} %param.19) | data formatting | bytes 16384 | tf_op jit(solution)/shard_map/reshape | solution.py:449
  2.7 2.4 %copy.14.router_hbm = bf16[4096,64]{1,0:T(8,128)(2,1)} copy(bf16[4096,64]{0,1:T(8,128)(2,1)} %param.20) | data formatting | bytes 1048576 | tf_op args[8]
  5.0 38.9 %shard_map.118 = bf16[1,16,64]{2,1,0:T(8,128)(2,1)} custom-call(bf16[1,16,4096]{2,1,0:T(8,128)(2,1)} %hidden_ref.1, bf16[1,1,16,128]{3,2,1,0:T(8,128)(2,1)} %query_ref.1, bf16[1,1,4096,128]{3,2,1,0:T(8,128)(2,1)} %key_hbm.1, bf16[1,1,4096,128]{3,2,1,0:T(8,128)(2,1)} %value_hbm.1, s32[1,16]{1,0:T(1,128)} %length_ref.1, s32[2,16,8]{2,1,0:T(8,128)} %copy.13.route_ref, ...), custom_call_target="tpu_custom_call" | custom-call | tf_op jit(solution)/shard_map/pallas_call | solution.py:402
  44.0 1.3 %copy.16 = bf16[1,16,64]{2,1,0:T(8,128)(2,1)} copy(bf16[1,16,64]{2,1,0:T(8,128)(2,1)} %shard_map.118) | data formatting | bytes 4096

commit v2 on v1

v2 whole, which is shorter than its diff:
```python
import functools

import jax
import jax.numpy as jnp
from jax import lax
from jax.experimental import pallas as pl
from jax.experimental.pallas import tpu as pltpu
from jax.sharding import PartitionSpec as P

MASKED_SCORE = -1e30
NORM_EPS = 1e-06
MESH = pl.DeviceIdType.MESH
LANES = 128
CAP = 4
SIDE = 4
PLANE = SIDE * SIDE
RING_ORDER = (2, 1, 3, 0)


def hops(step):
    return min(step, SIDE - step)


def far_first(steps):
    return sorted(steps, key=lambda step: -sum(hops(part) for part in step))


PLANE_STEPS = far_first([(dx, dy) for dx in range(SIDE) for dy in range(SIDE)])
CUBE_STEPS = far_first(
    [(dz, dx, dy) for dz in range(SIDE) for dx in range(SIDE) for dy in range(SIDE)]
)


def layer_kernel(
    hidden_hbm,
    query_hbm,
    key_hbm,
    value_hbm,
    length_hbm,
    route_hbm,
    out_weight_hbm,
    gain_hbm,
    router_hbm,
    gate_hbm,
    up_hbm,
    down_hbm,
    out_ref,
    hidden_ref,
    query_ref,
    length_ref,
    route_ref,
    gain_ref,
    key_buf,
    value_buf,
    out_weight_buf,
    router_buf,
    gate_buf,
    up_buf,
    down_buf,
    att_out,
    att_in,
    part_out,
    part_in,
    block_out,
    rows_in,
    gain_buf,
    inverse_buf,
    comb_out,
    comb_in,
    load_sem,
    att_send,
    att_recv,
    part_send,
    part_recv,
    rows_send,
    rows_recv,
    comb_send,
    comb_recv,
):
    s = lax.axis_index("sec")
    d = lax.axis_index("dev")
    z = d // PLANE
    x = lax.rem(d // SIDE, SIDE)
    y = lax.rem(d, SIDE)
    seqs = hidden_ref.shape[0]
    kv_span = key_buf.shape[0]
    head_dim = key_buf.shape[1]
    width = out_weight_buf.shape[1]
    rows = 2 * seqs
    chunk = width // SIDE
    chunk_blocks = chunk // LANES

    loads = [
        pltpu.make_async_copy(src, dst, load_sem.at[i])
        for i, (src, dst) in enumerate(
            (
                (length_hbm, length_ref),
                (query_hbm.at[0, 0], query_ref),
                (key_hbm.at[0, 0], key_buf),
                (value_hbm.at[0, 0], value_buf),
                (route_hbm, route_ref),
                (out_weight_hbm, out_weight_buf),
                (gate_hbm.at[0], gate_buf),
                (up_hbm.at[0], up_buf),
                (router_hbm, router_buf),
                (down_hbm.at[0], down_buf),
                (hidden_hbm.at[0], hidden_ref),
                (gain_hbm, gain_ref),
            )
        )
    ]
    (
        length_load,
        query_load,
        key_load,
        value_load,
        route_load,
        out_weight_load,
        gate_load,
        up_load,
        router_load,
        down_load,
        hidden_load,
        gain_load,
    ) = loads
    zs = [lax.rem(z + i, SIDE) for i in range(SIDE)]
    xs = [lax.rem(x + i, SIDE) for i in range(SIDE)]
    ys = [lax.rem(y + i, SIDE) for i in range(SIDE)]

    def at(dz, dx, dy):
        return zs[dz] * PLANE + xs[dx] * SIDE + ys[dy]

    barrier = pltpu.get_barrier_semaphore()

    def greet(target):
        pl.semaphore_signal(barrier, inc=1, device_id=(s, target), device_id_type=MESH)

    for load in loads[:4]:
        load.start()
    pl.semaphore_signal(barrier, inc=1, device_id=(1 - s, d), device_id_type=MESH)
    for dz, dx in PLANE_STEPS[:-1]:
        greet(zs[dz] * PLANE + xs[dx] * SIDE + z)
    for dx, turn in PLANE_STEPS:
        if turn:
            greet(y * PLANE + xs[dx] * SIDE + zs[turn])
    pl.when(y != z)(lambda: greet(z * PLANE + x * SIDE + z))
    for load in loads[4:]:
        load.start()

    query_load.wait()
    length_load.wait()
    key_load.wait()
    scores = lax.dot_general(
        query_ref[...], key_buf[...], (((1,), (1,)), ((), ())), preferred_element_type=jnp.float32
    ) * head_dim ** (-0.5)
    length = length_ref[0, d // SIDE]
    is_valid = lax.broadcasted_iota(jnp.int32, scores.shape, 1) < length
    scores = jnp.where(is_valid, scores, MASKED_SCORE)
    top = jnp.max(scores, axis=-1, keepdims=True)
    weights = jnp.where(is_valid, jnp.exp(scores - top), 0.0).astype(jnp.bfloat16)
    total = jnp.sum(weights.astype(jnp.float32), axis=-1, keepdims=True)
    value_load.wait()
    attended = jnp.dot(weights, value_buf[...], preferred_element_type=jnp.float32) / total
    att_out[...] = attended.reshape(att_out.shape)

    pl.semaphore_wait(barrier, 2 * PLANE - SIDE + 1 - (y == z).astype(jnp.int32))
    seq = d // SIDE
    for dx, dy in PLANE_STEPS:
        in_plane = xs[dx] * SIDE + ys[dy]
        src = att_out.at[in_plane]
        dst = att_in.at[seq]

        def send_row(src=src, dst=dst, target=y * PLANE + in_plane):
            pltpu.make_async_remote_copy(
                src, dst, att_send, att_recv, device_id=(s, target), device_id_type=MESH
            ).start()

        if (dx, dy) == (0, 0):
            pl.when(y != z)(send_row)

            @pl.when(y == z)
            def _():
                pltpu.make_async_copy(src, dst, att_recv).start()
        else:
            send_row()

    route_load.wait()
    routes = jnp.concatenate([route_ref[0], route_ref[1]], axis=1)
    chosen_row = jnp.sum((routes == d).astype(jnp.float32), axis=0, keepdims=True)
    row_a = lax.broadcasted_iota(jnp.int32, (rows, rows), 0)
    row_b = lax.broadcasted_iota(jnp.int32, (rows, rows), 1)
    before = (row_a < row_b) & (row_a // seqs == row_b // seqs)
    rank_row = jnp.dot(
        jnp.broadcast_to(chosen_row, (2 * CAP, rows)).astype(jnp.bfloat16),
        before.astype(jnp.bfloat16),
        preferred_element_type=jnp.float32,
    )
    slot = lax.broadcasted_iota(jnp.int32, (2 * CAP, rows), 0)
    token = lax.broadcasted_iota(jnp.int32, (2 * CAP, rows), 1)
    slot_batch = jnp.where(lax.rem(slot // 2, 2) == 0, s, 1 - s)
    slot_rank = slot // CAP * 2 + lax.rem(slot, 2)
    picked = (
        (token // seqs == slot_batch)
        & (rank_row == slot_rank.astype(jnp.float32))
        & (chosen_row > 0.5)
    )
    pick = jnp.where(picked, 1.0, 0.0).astype(jnp.bfloat16)

    experts = router_buf.shape[0]
    own_routes = route_ref[s]
    expert_row = lax.broadcasted_iota(jnp.int32, (experts, seqs), 0)
    match_rows = jnp.zeros((experts, seqs), jnp.float32)
    for k in range(own_routes.shape[0]):
        match_rows = match_rows + (own_routes[k : k + 1] == expert_row).astype(jnp.float32)
    same = lax.broadcasted_iota(jnp.int32, (seqs, seqs), 0) == lax.broadcasted_iota(
        jnp.int32, (seqs, seqs), 1
    )
    match = lax.dot_general(
        same.astype(jnp.bfloat16),
        match_rows.astype(jnp.bfloat16),
        (((1,), (1,)), ((), ())),
        preferred_element_type=jnp.float32,
    )
    lower = lax.broadcasted_iota(jnp.int32, (seqs, seqs), 0) > lax.broadcasted_iota(
        jnp.int32, (seqs, seqs), 1
    )
    rank = jnp.dot(
        lower.astype(jnp.bfloat16), match.astype(jnp.bfloat16), preferred_element_type=jnp.float32
    )
    slots = experts * 2
    spread = (
        lax.broadcasted_iota(jnp.int32, (experts, slots), 1) // 2
        == lax.broadcasted_iota(jnp.int32, (experts, slots), 0)
    ).astype(jnp.float32)
    rank_slots = jnp.dot(
        rank.astype(jnp.bfloat16), spread.astype(jnp.bfloat16), preferred_element_type=jnp.float32
    )
    low_slot = lax.rem(lax.broadcasted_iota(jnp.int32, (seqs, slots), 1), 2).astype(jnp.float32)
    in_slot = jnp.concatenate([rank_slots == low_slot, rank_slots == low_slot + 2.0], axis=0)

    out_weight_load.wait()
    pltpu.make_async_copy(att_in, att_in, att_recv).wait()
    head_rows = att_in[...].reshape(seqs, head_dim).astype(jnp.bfloat16)
    for dz in range(SIDE):
        base = pl.multiple_of(dz * chunk, chunk)
        partial = jnp.dot(
            head_rows, out_weight_buf[:, pl.ds(base, chunk)], preferred_element_type=jnp.float32
        ).astype(jnp.bfloat16)
        for j in range(chunk_blocks):
            part_out[dz * chunk_blocks + j] = partial[:, j * LANES : (j + 1) * LANES]
    for step in CUBE_STEPS:
        target = at(*step)
        src = part_out.at[target // 2]
        dst = part_in.at[d]
        if step == (0, 0, 0):
            pltpu.make_async_copy(src, dst, part_recv).start()
        else:
            pltpu.make_async_remote_copy(
                src, dst, part_send, part_recv, device_id=(s, target), device_id_type=MESH
            ).start()

    my_block = d // 2
    my_half = lax.rem(d, 2)
    lanes_at = pl.multiple_of(my_block * LANES, LANES)
    hidden_load.wait()
    gain_load.wait()
    hidden_block = hidden_ref[:, pl.ds(lanes_at, LANES)].astype(jnp.float32)
    gain = gain_ref[...].astype(jnp.float32)
    gain_buf[...] = gain
    inverse_buf[...] = 1.0 / (gain * gain)
    gain_block = gain_buf[pl.ds(my_block, 1), :]

    pltpu.make_async_copy(part_in, part_in, part_recv).wait()
    residual = hidden_block
    for i in range(part_in.shape[0]):
        residual = residual + part_in[i].astype(jnp.float32)
    block_out[...] = (residual * gain_block).astype(jnp.bfloat16)

    for step in CUBE_STEPS:
        dst = rows_in.at[my_block, s]

        def send_block(dst=dst, target=at(*step), dz=step[0]):
            pltpu.make_async_remote_copy(
                block_out,
                dst,
                rows_send,
                rows_recv.at[dz],
                device_id=(my_half, target),
                device_id_type=MESH,
            ).start()

        if step == (0, 0, 0):
            pl.when(my_half != s)(send_block)

            @pl.when(my_half == s)
            def _():
                pltpu.make_async_copy(block_out, dst, rows_recv.at[0]).start()
        else:
            send_block()

    gate_proj = jnp.zeros((2 * CAP, gate_buf.shape[1]), jnp.float32)
    up_proj = jnp.zeros((2 * CAP, gate_buf.shape[1]), jnp.float32)
    squares = jnp.zeros((2 * CAP, LANES), jnp.float32)
    gate_load.wait()
    up_load.wait()
    for dz in (0, 1, 3, 2):
        plane = lax.rem(z + SIDE - dz, SIDE)
        arrived = rows_in.at[pl.ds(plane * chunk_blocks, chunk_blocks)]
        pltpu.make_async_copy(arrived, arrived, rows_recv.at[dz]).wait()
        tokens = jnp.concatenate(
            [rows_in[plane * chunk_blocks + j].reshape(rows, LANES) for j in range(chunk_blocks)],
            axis=1,
        )
        picked_rows = jnp.dot(pick, tokens, preferred_element_type=jnp.float32)
        tokens = picked_rows.astype(jnp.bfloat16)
        base = pl.multiple_of(plane * chunk, chunk)
        gate_proj = gate_proj + jnp.dot(
            tokens, gate_buf[pl.ds(base, chunk), :], preferred_element_type=jnp.float32
        )
        up_proj = up_proj + jnp.dot(
            tokens, up_buf[pl.ds(base, chunk), :], preferred_element_type=jnp.float32
        )
        for j in range(chunk_blocks):
            wide = picked_rows[:, j * LANES : (j + 1) * LANES]
            row = plane * chunk_blocks + j
            squares = squares + wide * wide * inverse_buf[pl.ds(row, 1), :]
    scale = lax.rsqrt(jnp.sum(squares, axis=1, keepdims=True) / width + NORM_EPS)
    gate_proj = gate_proj * scale
    up_proj = up_proj * scale
    packed = (gate_proj * jax.nn.sigmoid(gate_proj) * up_proj).astype(jnp.bfloat16)

    down_load.wait()
    low_lane = lax.broadcasted_iota(jnp.int32, (CAP, LANES), 1) < LANES // 2

    def down():
        product = jnp.dot(packed, down_buf[...], preferred_element_type=jnp.float32)
        for j in range(chunk_blocks * SIDE):
            block = product[:, j * LANES : (j + 1) * LANES]
            turned = pltpu.roll(block, LANES // 2, 1)
            pair = (
                jnp.where(low_lane, block[:CAP], turned[CAP:]),
                jnp.where(low_lane, turned[:CAP], block[CAP:]),
            )
            for half in range(2):
                owner = j * 2 + half
                for batch in range(2):
                    comb_out[owner, batch] = pair[half][2 * batch : 2 * batch + 2]

    def combine(order):
        dz = RING_ORDER[order]
        for dx, dy in PLANE_STEPS:
            target = at(dz, dx, dy)
            dst = comb_in.at[s, d]
            for batch in (1, 0):
                src = comb_out.at[target, batch]
                if (dz, dx, dy, batch) == (0, 0, 0, 0):
                    pltpu.make_async_copy(src, dst, comb_recv).start()
                else:
                    group = s if batch == 0 else 1 - s
                    pltpu.make_async_remote_copy(
                        src, dst, comb_send, comb_recv, device_id=(group, target), device_id_type=MESH
                    ).start()

    down()
    for step in CUBE_STEPS:
        target = at(*step)
        dst = comb_in.at[s, d]
        for batch in (1, 0):
            src = comb_out.at[target, batch]
            if step == (0, 0, 0) and batch == 0:
                pltpu.make_async_copy(src, dst, comb_recv).start()
            else:
                group = s if batch == 0 else 1 - s
                pltpu.make_async_remote_copy(
                    src, dst, comb_send, comb_recv, device_id=(group, target), device_id_type=MESH
                ).start()

    router_load.wait()
    own_tokens = jnp.concatenate([rows_in[k, s] for k in range(rows_in.shape[0])], axis=1)
    own_squares = jnp.zeros((seqs, LANES), jnp.float32)
    for k in range(rows_in.shape[0]):
        wide = rows_in[k, s].astype(jnp.float32)
        own_squares = own_squares + wide * wide * inverse_buf[k : k + 1, :]
    own_scale = lax.rsqrt(jnp.sum(own_squares, axis=1, keepdims=True) / width + NORM_EPS)
    logits = lax.dot_general(
        own_tokens, router_buf[...], (((1,), (1,)), ((), ())), preferred_element_type=jnp.float32
    )
    shares = match * jax.nn.sigmoid(logits * own_scale)
    gates = shares / jnp.sum(shares, axis=1, keepdims=True)
    gate_slots = jnp.dot(
        gates, spread, precision=lax.Precision.HIGHEST, preferred_element_type=jnp.float32
    )
    gate_slots = jnp.where(in_slot, jnp.concatenate([gate_slots, gate_slots], axis=0), 0.0)

    pltpu.make_async_copy(comb_in, comb_in, comb_recv).wait()
    expert_rows = (comb_in[0] + comb_in[1]).reshape(slots, LANES)
    routed = jnp.dot(
        gate_slots,
        expert_rows,
        precision=lax.Precision.HIGHEST,
        preferred_element_type=jnp.float32,
    )
    features = out_ref.shape[2]
    mixed = jnp.where(my_half == 0, residual[:, :features], residual[:, features:])
    mixed = mixed + routed[:seqs, :features] + routed[seqs:, features:]
    out_ref[0] = mixed.astype(out_ref.dtype)

    most = att_in.at[pl.ds(0, PLANE - 1)]
    pltpu.make_async_copy(most, most, att_send).wait()

    @pl.when(y != z)
    def _():
        pltpu.make_async_copy(att_in.at[0], att_in.at[0], att_send).wait()

    most = part_in.at[pl.ds(0, SIDE * PLANE - 1)]
    pltpu.make_async_copy(most, most, part_send).wait()
    pltpu.make_async_copy(most, most, rows_send).wait()

    @pl.when(my_half != s)
    def _():
        pltpu.make_async_copy(block_out, block_out, rows_send).wait()

    pltpu.make_async_copy(comb_in.at[0], comb_in.at[0], comb_send).wait()
    most = comb_in.at[0, pl.ds(0, SIDE * PLANE - 1)]
    pltpu.make_async_copy(most, most, comb_send).wait()


def body(
    hidden_in,
    queries,
    key_cache,
    value_cache,
    kv_lengths,
    route_ids,
    out_weight,
    norm_gain,
    router_weight,
    w_gate,
    w_up,
    w_down,
):
    seqs, width = hidden_in.shape[1:]
    kv_span, head_dim = key_cache.shape[2:]
    experts = router_weight.shape[1]
    hidden_units = w_gate.shape[2]
    devices = lax.axis_size("dev")
    blocks = width // LANES
    vmem = pl.BlockSpec(memory_space=pltpu.VMEM)
    dma = pltpu.SemaphoreType.DMA
    return pl.pallas_call(
        layer_kernel,
        out_shape=jax.ShapeDtypeStruct((1, seqs, width // devices), jnp.bfloat16),
        in_specs=[pl.BlockSpec(memory_space=pl.ANY)] * 12,
        out_specs=vmem,
        scratch_shapes=[
            pltpu.VMEM((seqs, width), jnp.bfloat16),
            pltpu.VMEM(queries.shape[2:], jnp.bfloat16),
            pltpu.SMEM(kv_lengths.shape, jnp.int32),
            pltpu.VMEM((2, route_ids.shape[2], seqs), jnp.int32),
            pltpu.VMEM((blocks, LANES), jnp.bfloat16),
            pltpu.VMEM((kv_span, head_dim), jnp.bfloat16),
            pltpu.VMEM((kv_span, head_dim), jnp.bfloat16),
            pltpu.VMEM(out_weight.shape, jnp.bfloat16),
            pltpu.VMEM((experts, width), jnp.bfloat16),
            pltpu.VMEM((width, hidden_units), jnp.bfloat16),
            pltpu.VMEM((width, hidden_units), jnp.bfloat16),
            pltpu.VMEM((hidden_units, width), jnp.bfloat16),
            pltpu.VMEM((seqs, 1, head_dim), jnp.float32),
            pltpu.VMEM((seqs, 1, head_dim), jnp.float32),
            pltpu.VMEM((blocks, seqs, LANES), jnp.bfloat16),
            pltpu.VMEM((devices, seqs, LANES), jnp.bfloat16),
            pltpu.VMEM((seqs, LANES), jnp.bfloat16),
            pltpu.VMEM((blocks, 2, seqs, LANES), jnp.bfloat16),
            pltpu.VMEM((blocks, LANES), jnp.float32),
            pltpu.VMEM((blocks, LANES), jnp.float32),
            pltpu.VMEM((devices, 2, CAP // 2, LANES), jnp.float32),
            pltpu.VMEM((2, devices, CAP // 2, LANES), jnp.float32),
            dma((12,)),
            dma,
            dma,
            dma,
            dma,
            dma,
            dma((SIDE,)),
            dma,
            dma,
        ],
        compiler_params=pltpu.CompilerParams(
            collective_id=0, has_side_effects=True, vmem_limit_bytes=32 * 2**20
        ),
    )(*[
        pltpu.with_memory_space_constraint(operand, pltpu.HBM) for operand in (
        hidden_in,
        queries,
        key_cache,
        value_cache,
        kv_lengths,
        jnp.swapaxes(route_ids, 1, 2),
        out_weight,
        norm_gain.reshape(blocks, LANES),
        router_weight.T,
        w_gate,
        w_up,
        w_down,
    )])


def solution(mesh):
    placed = (
        P("sec", None, None),
        P("sec", "dev", None, None),
        P("sec", "dev", None, None),
        P("sec", "dev", None, None),
        P("sec", None),
        P(),
        P("dev", None),
        P(),
        P(),
        P("dev", None, "sec"),
        P("dev", None, "sec"),
        P("dev", "sec", None),
    )
    return jax.shard_map(
        body, mesh=mesh, in_specs=placed, out_specs=P("sec", None, "dev"), check_vma=False
    )
```

time: 45.5 us -> 37.4 us (0.82)
  local copies, waits for them, and re-layouts: 6.31 us -> 0.6 us
  Pallas kernels: 38.9 us -> 36.7 us
    unnamed x3 -> x1, local copies, waits for them, and re-layouts: 5.01 us -> 0.6 us
    pallas_call x1, Pallas kernels: 38.9 us -> 36.7 us  [body(): pl.pallas_call(layer_kernel, out_shape=jax.ShapeDtypeStruct((1, seqs, wid...]
    reshape x1 -> x0, local copies, waits for them, and re-layouts: 1.3 us -> none  [body(): norm_gain.reshape(1, width)]
where the time goes in v2:
time: 37.4 us; the launch traced here: 37.3 us
  Pallas kernels  36.7 us (98%)
  local copies, waits for them, and re-layouts  0.6 us (2%)
    pallas_call x1, Pallas kernels, body(): pl.pallas_call(layer_kernel, out_shape=jax.ShapeDtypeStruct((1, seqs, wid...  36.7 us

profile of v2, /device:TPU:1, one launch (start us, length us, event | category | flops | bytes accessed | tf_op | source)
XLA Modules:
  0.0 37.3 jit_solution(14287300210099454580)
XLA Ops:
  0.0 36.7 %shard_map.118 = bf16[1,16,64]{2,1,0:T(8,128)(2,1)S(1)} custom-call(bf16[1,16,4096]{2,1,0:T(8,128)(2,1)} %hidden_hbm.1, bf16[1,1,16,128]{3,2,1,0:T(8,128)(2,1)} %query_hbm.1, bf16[1,1,4096,128]{3,2,1,0:T(8,128)(2,1)} %key_hbm.1, bf16[1,1,4096,128]{3,2,1,0:T(8,128)(2,1)} %value_hbm.1, s32[1,16]{1,0:T(1,128)} %length_hbm.1, s32[2,8,16]{2,1,0:T(8,128)} %bitcast.4, ...), custom_call_target="tpu_custom_call" | custom-call | tf_op jit(solution)/shard_map/pallas_call | solution.py:450
  36.7 0.6 %copy.14 = bf16[1,16,64]{2,1,0:T(8,128)(2,1)} copy(bf16[1,16,64]{2,1,0:T(8,128)(2,1)S(1)} %shard_map.118) | data formatting | bytes 4096

commit v3 on v2

--- a/solution.py
+++ b/solution.py
@@ -184,59 +184,62 @@
         else:
             send_row()
 
+    experts = router_buf.shape[0]
     route_load.wait()
+
+    def match_of(routes):
+        expert_row = lax.broadcasted_iota(jnp.int32, (experts, routes.shape[1]), 0)
+        match = jnp.zeros(expert_row.shape, jnp.float32)
+        for k in range(routes.shape[0]):
+            match = match + (routes[k : k + 1] == expert_row).astype(jnp.float32)
+        return match.astype(jnp.bfloat16)
+
+    def exact_dot(left, right, left_dim=1, right_dim=0):
+        return lax.dot_general(
+            left.astype(jnp.bfloat16),
+            right.astype(jnp.bfloat16),
+            (((left_dim,), (right_dim,)), ((), ())),
+            preferred_element_type=jnp.float32,
+        )
+
+    def iota(shape, dim):
+        return lax.broadcasted_iota(jnp.int32, shape, dim)
+
     routes = jnp.concatenate([route_ref[0], route_ref[1]], axis=1)
     chosen_row = jnp.sum((routes == d).astype(jnp.float32), axis=0, keepdims=True)
-    row_a = lax.broadcasted_iota(jnp.int32, (rows, rows), 0)
-    row_b = lax.broadcasted_iota(jnp.int32, (rows, rows), 1)
+    row_a, row_b = iota((rows, rows), 0), iota((rows, rows), 1)
     before = (row_a < row_b) & (row_a // seqs == row_b // seqs)
-    rank_row = jnp.dot(
-        jnp.broadcast_to(chosen_row, (2 * CAP, rows)).astype(jnp.bfloat16),
-        before.astype(jnp.bfloat16),
-        preferred_element_type=jnp.float32,
-    )
-    slot = lax.broadcasted_iota(jnp.int32, (2 * CAP, rows), 0)
-    token = lax.broadcasted_iota(jnp.int32, (2 * CAP, rows), 1)
-    slot_batch = jnp.where(lax.rem(slot // 2, 2) == 0, s, 1 - s)
-    slot_rank = slot // CAP * 2 + lax.rem(slot, 2)
-    picked = (
-        (token // seqs == slot_batch)
-        & (rank_row == slot_rank.astype(jnp.float32))
+    rank_row = exact_dot(jnp.broadcast_to(chosen_row, (2 * CAP, rows)), before)
+    slot, token = iota((2 * CAP, rows), 0), iota((2 * CAP, rows), 1)
+    pick = (
+        (token // seqs == slot // CAP)
+        & (rank_row == lax.rem(slot, CAP).astype(jnp.float32))
         & (chosen_row > 0.5)
     )
-    pick = jnp.where(picked, 1.0, 0.0).astype(jnp.bfloat16)
-
-    experts = router_buf.shape[0]
-    own_routes = route_ref[s]
-    expert_row = lax.broadcasted_iota(jnp.int32, (experts, seqs), 0)
-    match_rows = jnp.zeros((experts, seqs), jnp.float32)
-    for k in range(own_routes.shape[0]):
-        match_rows = match_rows + (own_routes[k : k + 1] == expert_row).astype(jnp.float32)
-    same = lax.broadcasted_iota(jnp.int32, (seqs, seqs), 0) == lax.broadcasted_iota(
-        jnp.int32, (seqs, seqs), 1
-    )
-    match = lax.dot_general(
-        same.astype(jnp.bfloat16),
-        match_rows.astype(jnp.bfloat16),
-        (((1,), (1,)), ((), ())),
-        preferred_element_type=jnp.float32,
-    )
-    lower = lax.broadcasted_iota(jnp.int32, (seqs, seqs), 0) > lax.broadcasted_iota(
-        jnp.int32, (seqs, seqs), 1
-    )
-    rank = jnp.dot(
-        lower.astype(jnp.bfloat16), match.astype(jnp.bfloat16), preferred_element_type=jnp.float32
-    )
+    chosen = exact_dot(pick, match_of(routes), 1, 1)
+
+    match_rows = match_of(route_ref[s])
+    token_a, token_b = iota((seqs, seqs), 0), iota((seqs, seqs), 1)
+    rank_rows = exact_dot(match_rows, token_a < token_b)
+    wide = experts * CAP
+    to_slots = iota((wide, experts), 0) // CAP == iota((wide, experts), 1)
+    gather_rows = (exact_dot(to_slots, match_rows) > 0.5) & (
+        exact_dot(to_slots, rank_rows) == lax.rem(iota((wide, seqs), 0), CAP).astype(jnp.float32)
+    )
+    match = exact_dot(token_a == token_b, match_rows, 1, 1)
+    rank = exact_dot(token_a == token_b, rank_rows, 1, 1)
     slots = experts * 2
-    spread = (
-        lax.broadcasted_iota(jnp.int32, (experts, slots), 1) // 2
-        == lax.broadcasted_iota(jnp.int32, (experts, slots), 0)
-    ).astype(jnp.float32)
-    rank_slots = jnp.dot(
-        rank.astype(jnp.bfloat16), spread.astype(jnp.bfloat16), preferred_element_type=jnp.float32
-    )
-    low_slot = lax.rem(lax.broadcasted_iota(jnp.int32, (seqs, slots), 1), 2).astype(jnp.float32)
-    in_slot = jnp.concatenate([rank_slots == low_slot, rank_slots == low_slot + 2.0], axis=0)
+    spread = iota((experts, slots), 1) // 2 == iota((experts, slots), 0)
+    match_slots = exact_dot(match, spread) > 0.5
+    rank_slots = exact_dot(rank, spread)
+    low_slot = lax.rem(iota((seqs, slots), 1), 2).astype(jnp.float32)
+    scatter_rows = jnp.concatenate(
+        [
+            jnp.where(match_slots & (rank_slots == low_slot + 2.0 * i), 1.0, 0.0)
+            for i in range(CAP // 2)
+        ],
+        axis=0,
+    )
 
     out_weight_load.wait()
     pltpu.make_async_copy(att_in, att_in, att_recv).wait()
@@ -274,14 +277,18 @@
     residual = hidden_block
     for i in range(part_in.shape[0]):
         residual = residual + part_in[i].astype(jnp.float32)
-    block_out[...] = (residual * gain_block).astype(jnp.bfloat16)
+    block = (residual * gain_block).astype(jnp.bfloat16)
+    block_rows = exact_dot(gather_rows, block)
+    for e in range(experts):
+        block_out[e] = block_rows[e * CAP : (e + 1) * CAP]
 
     for step in CUBE_STEPS:
+        src = block_out.at[at(*step)]
         dst = rows_in.at[my_block, s]
 
-        def send_block(dst=dst, target=at(*step), dz=step[0]):
+        def send_block(src=src, dst=dst, target=at(*step), dz=step[0]):
             pltpu.make_async_remote_copy(
-                block_out,
+                src,
                 dst,
                 rows_send,
                 rows_recv.at[dz],
@@ -294,24 +301,28 @@
 
             @pl.when(my_half == s)
             def _():
-                pltpu.make_async_copy(block_out, dst, rows_recv.at[0]).start()
+                pltpu.make_async_copy(src, dst, rows_recv.at[0]).start()
         else:
             send_block()
 
     gate_proj = jnp.zeros((2 * CAP, gate_buf.shape[1]), jnp.float32)
     up_proj = jnp.zeros((2 * CAP, gate_buf.shape[1]), jnp.float32)
     squares = jnp.zeros((2 * CAP, LANES), jnp.float32)
+    logits = jnp.zeros((2 * CAP, experts), jnp.float32)
+    router_load.wait()
     gate_load.wait()
     up_load.wait()
     for dz in (0, 1, 3, 2):
         plane = lax.rem(z + SIDE - dz, SIDE)
         arrived = rows_in.at[pl.ds(plane * chunk_blocks, chunk_blocks)]
         pltpu.make_async_copy(arrived, arrived, rows_recv.at[dz]).wait()
-        tokens = jnp.concatenate(
-            [rows_in[plane * chunk_blocks + j].reshape(rows, LANES) for j in range(chunk_blocks)],
+        picked_rows = jnp.concatenate(
+            [
+                rows_in[plane * chunk_blocks + j].reshape(2 * CAP, LANES)
+                for j in range(chunk_blocks)
+            ],
             axis=1,
         )
-        picked_rows = jnp.dot(pick, tokens, preferred_element_type=jnp.float32)
         tokens = picked_rows.astype(jnp.bfloat16)
         base = pl.multiple_of(plane * chunk, chunk)
         gate_proj = gate_proj + jnp.dot(
@@ -319,83 +330,76 @@
         )
         up_proj = up_proj + jnp.dot(
             tokens, up_buf[pl.ds(base, chunk), :], preferred_element_type=jnp.float32
+        )
+        logits = logits + lax.dot_general(
+            tokens,
+            router_buf[:, pl.ds(base, chunk)],
+            (((1,), (1,)), ((), ())),
+            preferred_element_type=jnp.float32,
         )
         for j in range(chunk_blocks):
             wide = picked_rows[:, j * LANES : (j + 1) * LANES]
             row = plane * chunk_blocks + j
             squares = squares + wide * wide * inverse_buf[pl.ds(row, 1), :]
     scale = lax.rsqrt(jnp.sum(squares, axis=1, keepdims=True) / width + NORM_EPS)
+    shares = chosen * jax.nn.sigmoid(logits * scale)
+    share_sum = jnp.sum(shares, axis=1, keepdims=True)
+    own_share = jnp.sum(
+        jnp.where(iota(shares.shape, 1) == d, shares, 0.0), axis=1, keepdims=True
+    )
+    gates = jnp.where(share_sum > 0.0, own_share / share_sum, 0.0)
     gate_proj = gate_proj * scale
     up_proj = up_proj * scale
     packed = (gate_proj * jax.nn.sigmoid(gate_proj) * up_proj).astype(jnp.bfloat16)
 
     down_load.wait()
-    low_lane = lax.broadcasted_iota(jnp.int32, (CAP, LANES), 1) < LANES // 2
-
-    def down():
-        product = jnp.dot(packed, down_buf[...], preferred_element_type=jnp.float32)
-        for j in range(chunk_blocks * SIDE):
+    low_lane = iota((CAP // 2, LANES), 1) < LANES // 2
+
+    def down(plane):
+        product = gates * jnp.dot(
+            packed,
+            down_buf[:, plane * chunk : (plane + 1) * chunk],
+            preferred_element_type=jnp.float32,
+        )
+        for j in range(chunk_blocks):
             block = product[:, j * LANES : (j + 1) * LANES]
             turned = pltpu.roll(block, LANES // 2, 1)
-            pair = (
-                jnp.where(low_lane, block[:CAP], turned[CAP:]),
-                jnp.where(low_lane, turned[:CAP], block[CAP:]),
-            )
-            for half in range(2):
-                owner = j * 2 + half
-                for batch in range(2):
-                    comb_out[owner, batch] = pair[half][2 * batch : 2 * batch + 2]
-
-    def combine(order):
-        dz = RING_ORDER[order]
+            owner = plane * PLANE + j * 2
+            for batch in range(2):
+                low = slice(batch * CAP, batch * CAP + CAP // 2)
+                high = slice(batch * CAP + CAP // 2, (batch + 1) * CAP)
+                comb_out[owner, batch] = jnp.where(low_lane, block[low], turned[high])
+                comb_out[owner + 1, batch] = jnp.where(low_lane, turned[low], block[high])
+
+    def combine(plane):
         for dx, dy in PLANE_STEPS:
-            target = at(dz, dx, dy)
+            target = plane * PLANE + xs[dx] * SIDE + ys[dy]
             dst = comb_in.at[s, d]
-            for batch in (1, 0):
-                src = comb_out.at[target, batch]
-                if (dz, dx, dy, batch) == (0, 0, 0, 0):
-                    pltpu.make_async_copy(src, dst, comb_recv).start()
-                else:
-                    group = s if batch == 0 else 1 - s
+            for group in (1 - s, s):
+                src = comb_out.at[target, group]
+
+                def send_rows(src=src, dst=dst, group=group, target=target):
                     pltpu.make_async_remote_copy(
                         src, dst, comb_send, comb_recv, device_id=(group, target), device_id_type=MESH
                     ).start()
 
-    down()
-    for step in CUBE_STEPS:
-        target = at(*step)
-        dst = comb_in.at[s, d]
-        for batch in (1, 0):
-            src = comb_out.at[target, batch]
-            if step == (0, 0, 0) and batch == 0:
-                pltpu.make_async_copy(src, dst, comb_recv).start()
-            else:
-                group = s if batch == 0 else 1 - s
-                pltpu.make_async_remote_copy(
-                    src, dst, comb_send, comb_recv, device_id=(group, target), device_id_type=MESH
-                ).start()
-
-    router_load.wait()
-    own_tokens = jnp.concatenate([rows_in[k, s] for k in range(rows_in.shape[0])], axis=1)
-    own_squares = jnp.zeros((seqs, LANES), jnp.float32)
-    for k in range(rows_in.shape[0]):
-        wide = rows_in[k, s].astype(jnp.float32)
-        own_squares = own_squares + wide * wide * inverse_buf[k : k + 1, :]
-    own_scale = lax.rsqrt(jnp.sum(own_squares, axis=1, keepdims=True) / width + NORM_EPS)
-    logits = lax.dot_general(
-        own_tokens, router_buf[...], (((1,), (1,)), ((), ())), preferred_element_type=jnp.float32
-    )
-    shares = match * jax.nn.sigmoid(logits * own_scale)
-    gates = shares / jnp.sum(shares, axis=1, keepdims=True)
-    gate_slots = jnp.dot(
-        gates, spread, precision=lax.Precision.HIGHEST, preferred_element_type=jnp.float32
-    )
-    gate_slots = jnp.where(in_slot, jnp.concatenate([gate_slots, gate_slots], axis=0), 0.0)
+                if (dx, dy) == (0, 0) and group is s:
+                    pl.when(z != plane)(send_rows)
+
+                    @pl.when(z == plane)
+                    def _(src=src, dst=dst):
+                        pltpu.make_async_copy(src, dst, comb_recv).start()
+                else:
+                    send_rows()
+
+    for plane in (0, 1, 3, 2):
+        down(plane)
+        combine(plane)
 
     pltpu.make_async_copy(comb_in, comb_in, comb_recv).wait()
     expert_rows = (comb_in[0] + comb_in[1]).reshape(slots, LANES)
     routed = jnp.dot(
-        gate_slots,
+        scatter_rows,
         expert_rows,
         precision=lax.Precision.HIGHEST,
         preferred_element_type=jnp.float32,
@@ -414,11 +418,12 @@
 
     most = part_in.at[pl.ds(0, SIDE * PLANE - 1)]
     pltpu.make_async_copy(most, most, part_send).wait()
+    most = block_out.at[pl.ds(0, SIDE * PLANE - 1)]
     pltpu.make_async_copy(most, most, rows_send).wait()
 
     @pl.when(my_half != s)
     def _():
-        pltpu.make_async_copy(block_out, block_out, rows_send).wait()
+        pltpu.make_async_copy(block_out.at[0], block_out.at[0], rows_send).wait()
 
     pltpu.make_async_copy(comb_in.at[0], comb_in.at[0], comb_send).wait()
     most = comb_in.at[0, pl.ds(0, SIDE * PLANE - 1)]
@@ -469,8 +474,8 @@
             pltpu.VMEM((seqs, 1, head_dim), jnp.float32),
             pltpu.VMEM((blocks, seqs, LANES), jnp.bfloat16),
             pltpu.VMEM((devices, seqs, LANES), jnp.bfloat16),
-            pltpu.VMEM((seqs, LANES), jnp.bfloat16),
-            pltpu.VMEM((blocks, 2, seqs, LANES), jnp.bfloat16),
+            pltpu.VMEM((experts, CAP, LANES), jnp.float32),
+            pltpu.VMEM((blocks, 2, CAP, LANES), jnp.float32),
             pltpu.VMEM((blocks, LANES), jnp.float32),
             pltpu.VMEM((blocks, LANES), jnp.float32),
             pltpu.VMEM((devices, 2, CAP // 2, LANES), jnp.float32),

time: 37.4 us -> 36.4 us (0.973)
  Pallas kernels: 36.7 us -> 35.7 us
    pallas_call x1, Pallas kernels: 36.7 us -> 35.7 us  [body(): pl.pallas_call(layer_kernel, out_shape=jax.ShapeDtypeStruct((1, seqs, wid...]
where the time goes in v3:
time: 36.4 us; the launch traced here: 36.3 us
  Pallas kernels  35.7 us (98%)
  local copies, waits for them, and re-layouts  0.6 us (2%)
    pallas_call x1, Pallas kernels, body(): pl.pallas_call(layer_kernel, out_shape=jax.ShapeDtypeStruct((1, seqs, wid...  35.7 us

profile of v3, /device:TPU:1, one launch (start us, length us, event | category | flops | bytes accessed | tf_op | source)
XLA Modules:
  0.0 36.3 jit_solution(5573843152904130873)
XLA Ops:
  0.0 35.7 %shard_map.118 = bf16[1,16,64]{2,1,0:T(8,128)(2,1)S(1)} custom-call(bf16[1,16,4096]{2,1,0:T(8,128)(2,1)} %hidden_hbm.1, bf16[1,1,16,128]{3,2,1,0:T(8,128)(2,1)} %query_hbm.1, bf16[1,1,4096,128]{3,2,1,0:T(8,128)(2,1)} %key_hbm.1, bf16[1,1,4096,128]{3,2,1,0:T(8,128)(2,1)} %value_hbm.1, s32[1,16]{1,0:T(1,128)} %length_hbm.1, s32[2,8,16]{2,1,0:T(8,128)} %bitcast.4, ...), custom_call_target="tpu_custom_call" | custom-call | tf_op jit(solution)/shard_map/pallas_call | solution.py:455
  35.7 0.6 %copy.14 = bf16[1,16,64]{2,1,0:T(8,128)(2,1)} copy(bf16[1,16,64]{2,1,0:T(8,128)(2,1)S(1)} %shard_map.118) | data formatting | bytes 4096

commit v4 on v3

--- a/solution.py
+++ b/solution.py
@@ -1,5 +1,3 @@
-import functools
-
 import jax
 import jax.numpy as jnp
 from jax import lax
@@ -14,7 +12,7 @@
 CAP = 4
 SIDE = 4
 PLANE = SIDE * SIDE
-RING_ORDER = (2, 1, 3, 0)
+BATCH = 4
 
 
 def hops(step):
@@ -29,6 +27,12 @@
 CUBE_STEPS = far_first(
     [(dz, dx, dy) for dz in range(SIDE) for dx in range(SIDE) for dy in range(SIDE)]
 )
+
+NEAR_STEPS = [
+    (dz, dx, dy)
+    for dz, dx, dy in CUBE_STEPS[::-1]
+    if hops(dz) + hops(dx) + hops(dy) < hops((dz + 2) % 4) + hops((dx + 2) % 4) + hops((dy + 3) % 4)
+]
 
 
 def layer_kernel(
@@ -65,6 +69,8 @@
     rows_in,
     gain_buf,
     inverse_buf,
+    res_out,
+    res_in,
     comb_out,
     comb_in,
     load_sem,
@@ -74,6 +80,8 @@
     part_recv,
     rows_send,
     rows_recv,
+    res_send,
+    res_recv,
     comb_send,
     comb_recv,
 ):
@@ -83,7 +91,6 @@
     x = lax.rem(d // SIDE, SIDE)
     y = lax.rem(d, SIDE)
     seqs = hidden_ref.shape[0]
-    kv_span = key_buf.shape[0]
     head_dim = key_buf.shape[1]
     width = out_weight_buf.shape[1]
     rows = 2 * seqs
@@ -251,9 +258,18 @@
         ).astype(jnp.bfloat16)
         for j in range(chunk_blocks):
             part_out[dz * chunk_blocks + j] = partial[:, j * LANES : (j + 1) * LANES]
+    odd = lax.rem(y, 2)
+    shifts = (2 * odd, 2 * (1 - odd))
+    block_z = [[lax.rem(z + i + shift, SIDE) for i in range(SIDE)] for shift in shifts]
+    block_x = [[lax.rem(x + i + shift, SIDE) for i in range(SIDE)] for shift in shifts]
+
+    def block_at(dz, dx, dy):
+        place = block_z[dy % 2][dz] * SIDE + block_x[dy % 2][dx]
+        return place * 2 + ys[dy] // 2
+
     for step in CUBE_STEPS:
         target = at(*step)
-        src = part_out.at[target // 2]
+        src = part_out.at[block_at(*step)]
         dst = part_in.at[d]
         if step == (0, 0, 0):
             pltpu.make_async_copy(src, dst, part_recv).start()
@@ -262,8 +278,7 @@
                 src, dst, part_send, part_recv, device_id=(s, target), device_id_type=MESH
             ).start()
 
-    my_block = d // 2
-    my_half = lax.rem(d, 2)
+    my_block = block_at(0, 0, 0)
     lanes_at = pl.multiple_of(my_block * LANES, LANES)
     hidden_load.wait()
     gain_load.wait()
@@ -282,28 +297,32 @@
     for e in range(experts):
         block_out[e] = block_rows[e * CAP : (e + 1) * CAP]
 
-    for step in CUBE_STEPS:
-        src = block_out.at[at(*step)]
-        dst = rows_in.at[my_block, s]
-
-        def send_block(src=src, dst=dst, target=at(*step), dz=step[0]):
-            pltpu.make_async_remote_copy(
-                src,
-                dst,
-                rows_send,
-                rows_recv.at[dz],
-                device_id=(my_half, target),
-                device_id_type=MESH,
-            ).start()
-
-        if step == (0, 0, 0):
-            pl.when(my_half != s)(send_block)
-
-            @pl.when(my_half == s)
-            def _():
-                pltpu.make_async_copy(src, dst, rows_recv.at[0]).start()
-        else:
-            send_block()
+    turn = 1 - 2 * odd
+    near_z = [lax.rem(z + turn * i + SIDE, SIDE) for i in range(SIDE)]
+    near_x = [lax.rem(x + turn * i + SIDE, SIDE) for i in range(SIDE)]
+    near_y = [lax.rem(y + turn * i + SIDE, SIDE) for i in range(SIDE)]
+    for place, (dz, dx, dy) in enumerate(NEAR_STEPS):
+        target = near_z[dz] * PLANE + near_x[dx] * SIDE + near_y[dy]
+        src = block_out.at[target]
+        dst = rows_in.at[place, s]
+        arrival = rows_recv.at[place // BATCH]
+        for group in (1 - s, s):
+            if (dz, dx, dy) == (0, 0, 0) and group is s:
+                pltpu.make_async_copy(src, dst, arrival).start()
+            else:
+                pltpu.make_async_remote_copy(
+                    src, dst, rows_send, arrival, device_id=(group, target), device_id_type=MESH
+                ).start()
+
+    res_out[...] = residual
+    res_copy = pltpu.make_async_remote_copy(
+        res_out, res_in, res_send, res_recv, device_id=(s, d + turn), device_id_type=MESH
+    )
+
+    @pl.when(odd == 0)
+    def _():
+        res_in[...] = residual
+        res_copy.start()
 
     gate_proj = jnp.zeros((2 * CAP, gate_buf.shape[1]), jnp.float32)
     up_proj = jnp.zeros((2 * CAP, gate_buf.shape[1]), jnp.float32)
@@ -312,35 +331,35 @@
     router_load.wait()
     gate_load.wait()
     up_load.wait()
-    for dz in (0, 1, 3, 2):
-        plane = lax.rem(z + SIDE - dz, SIDE)
-        arrived = rows_in.at[pl.ds(plane * chunk_blocks, chunk_blocks)]
-        pltpu.make_async_copy(arrived, arrived, rows_recv.at[dz]).wait()
-        picked_rows = jnp.concatenate(
-            [
-                rows_in[plane * chunk_blocks + j].reshape(2 * CAP, LANES)
-                for j in range(chunk_blocks)
-            ],
-            axis=1,
-        )
+    def from_steps(center, shift, side):
+        return [lax.rem(center + SIDE - (1 - 2 * side) * i + shift * side, SIDE) for i in range(SIDE)]
+
+    sides = (odd, 1 - odd)
+    from_z = [from_steps(z, 2, side) for side in sides]
+    from_x = [from_steps(x, 2, side) for side in sides]
+    from_y = [from_steps(y, 0, side) for side in sides]
+    for place, (dz, dx, dy) in enumerate(NEAR_STEPS):
+        if place % BATCH == 0:
+            arrived = rows_in.at[pl.ds(place, BATCH)]
+            pltpu.make_async_copy(arrived, arrived, rows_recv.at[place // BATCH]).wait()
+        side = dy % 2
+        row = (from_z[side][dz] * SIDE + from_x[side][dx]) * 2 + from_y[side][dy] // 2
+        base = pl.multiple_of(row * LANES, LANES)
+        picked_rows = rows_in[place].reshape(2 * CAP, LANES)
         tokens = picked_rows.astype(jnp.bfloat16)
-        base = pl.multiple_of(plane * chunk, chunk)
         gate_proj = gate_proj + jnp.dot(
-            tokens, gate_buf[pl.ds(base, chunk), :], preferred_element_type=jnp.float32
+            tokens, gate_buf[pl.ds(base, LANES), :], preferred_element_type=jnp.float32
         )
         up_proj = up_proj + jnp.dot(
-            tokens, up_buf[pl.ds(base, chunk), :], preferred_element_type=jnp.float32
+            tokens, up_buf[pl.ds(base, LANES), :], preferred_element_type=jnp.float32
         )
         logits = logits + lax.dot_general(
             tokens,
-            router_buf[:, pl.ds(base, chunk)],
+            router_buf[:, pl.ds(base, LANES)],
             (((1,), (1,)), ((), ())),
             preferred_element_type=jnp.float32,
         )
-        for j in range(chunk_blocks):
-            wide = picked_rows[:, j * LANES : (j + 1) * LANES]
-            row = plane * chunk_blocks + j
-            squares = squares + wide * wide * inverse_buf[pl.ds(row, 1), :]
+        squares = squares + picked_rows * picked_rows * inverse_buf[pl.ds(row, 1), :]
     scale = lax.rsqrt(jnp.sum(squares, axis=1, keepdims=True) / width + NORM_EPS)
     shares = chosen * jax.nn.sigmoid(logits * scale)
     share_sum = jnp.sum(shares, axis=1, keepdims=True)
@@ -405,7 +424,9 @@
         preferred_element_type=jnp.float32,
     )
     features = out_ref.shape[2]
-    mixed = jnp.where(my_half == 0, residual[:, :features], residual[:, features:])
+    pl.when(odd == 1)(res_copy.wait_recv)
+    residual = res_in[...]
+    mixed = jnp.where(odd == 0, residual[:, :features], residual[:, features:])
     mixed = mixed + routed[:seqs, :features] + routed[seqs:, features:]
     out_ref[0] = mixed.astype(out_ref.dtype)
 
@@ -420,10 +441,7 @@
     pltpu.make_async_copy(most, most, part_send).wait()
     most = block_out.at[pl.ds(0, SIDE * PLANE - 1)]
     pltpu.make_async_copy(most, most, rows_send).wait()
-
-    @pl.when(my_half != s)
-    def _():
-        pltpu.make_async_copy(block_out.at[0], block_out.at[0], rows_send).wait()
+    pl.when(odd == 0)(res_copy.wait_send)
 
     pltpu.make_async_copy(comb_in.at[0], comb_in.at[0], comb_send).wait()
     most = comb_in.at[0, pl.ds(0, SIDE * PLANE - 1)]
@@ -450,13 +468,26 @@
     hidden_units = w_gate.shape[2]
     devices = lax.axis_size("dev")
     blocks = width // LANES
-    vmem = pl.BlockSpec(memory_space=pltpu.VMEM)
+    operands = (
+        hidden_in,
+        queries,
+        key_cache,
+        value_cache,
+        kv_lengths,
+        jnp.swapaxes(route_ids, 1, 2),
+        out_weight,
+        norm_gain.reshape(blocks, LANES),
+        router_weight.T,
+        w_gate,
+        w_up,
+        w_down,
+    )
     dma = pltpu.SemaphoreType.DMA
     return pl.pallas_call(
         layer_kernel,
         out_shape=jax.ShapeDtypeStruct((1, seqs, width // devices), jnp.bfloat16),
-        in_specs=[pl.BlockSpec(memory_space=pl.ANY)] * 12,
-        out_specs=vmem,
+        in_specs=[pl.BlockSpec(memory_space=pl.ANY)] * len(operands),
+        out_specs=pl.BlockSpec(memory_space=pltpu.VMEM),
         scratch_shapes=[
             pltpu.VMEM((seqs, width), jnp.bfloat16),
             pltpu.VMEM(queries.shape[2:], jnp.bfloat16),
@@ -478,6 +509,8 @@
             pltpu.VMEM((blocks, 2, CAP, LANES), jnp.float32),
             pltpu.VMEM((blocks, LANES), jnp.float32),
             pltpu.VMEM((blocks, LANES), jnp.float32),
+            pltpu.VMEM((seqs, LANES), jnp.float32),
+            pltpu.VMEM((seqs, LANES), jnp.float32),
             pltpu.VMEM((devices, 2, CAP // 2, LANES), jnp.float32),
             pltpu.VMEM((2, devices, CAP // 2, LANES), jnp.float32),
             dma((12,)),
@@ -486,28 +519,16 @@
             dma,
             dma,
             dma,
-            dma((SIDE,)),
+            dma((blocks // BATCH,)),
+            dma,
+            dma,
             dma,
             dma,
         ],
         compiler_params=pltpu.CompilerParams(
             collective_id=0, has_side_effects=True, vmem_limit_bytes=32 * 2**20
         ),
-    )(*[
-        pltpu.with_memory_space_constraint(operand, pltpu.HBM) for operand in (
-        hidden_in,
-        queries,
-        key_cache,
-        value_cache,
-        kv_lengths,
-        jnp.swapaxes(route_ids, 1, 2),
-        out_weight,
-        norm_gain.reshape(blocks, LANES),
-        router_weight.T,
-        w_gate,
-        w_up,
-        w_down,
-    )])
+    )(*[pltpu.with_memory_space_constraint(operand, pltpu.HBM) for operand in operands])
 
 
 def solution(mesh):

time: 36.4 us -> 35.6 us (0.978)
  Pallas kernels: 35.7 us -> 34.9 us
    pallas_call x1, Pallas kernels: 35.7 us -> 34.9 us  [body(): pl.pallas_call(layer_kernel, out_shape=jax.ShapeDtypeStruct((1, seqs, wid...]
where the time goes in v4:
time: 35.6 us; the launch traced here: 35.5 us
  Pallas kernels  34.9 us (98%)
  local copies, waits for them, and re-layouts  0.6 us (2%)
    pallas_call x1, Pallas kernels, body(): pl.pallas_call(layer_kernel, out_shape=jax.ShapeDtypeStruct((1, seqs, wid...  34.9 us

profile of v4, /device:TPU:1, one launch (start us, length us, event | category | flops | bytes accessed | tf_op | source)
XLA Modules:
  0.0 35.5 jit_solution(9863364188011475288)
XLA Ops:
  0.0 34.9 %shard_map.118 = bf16[1,16,64]{2,1,0:T(8,128)(2,1)S(1)} custom-call(bf16[1,16,4096]{2,1,0:T(8,128)(2,1)} %hidden_hbm.1, bf16[1,1,16,128]{3,2,1,0:T(8,128)(2,1)} %query_hbm.1, bf16[1,1,4096,128]{3,2,1,0:T(8,128)(2,1)} %key_hbm.1, bf16[1,1,4096,128]{3,2,1,0:T(8,128)(2,1)} %value_hbm.1, s32[1,16]{1,0:T(1,128)} %length_hbm.1, s32[2,8,16]{2,1,0:T(8,128)} %bitcast.4, ...), custom_call_target="tpu_custom_call" | custom-call | tf_op jit(solution)/shard_map/pallas_call | solution.py:486
  34.9 0.6 %copy.14 = bf16[1,16,64]{2,1,0:T(8,128)(2,1)} copy(bf16[1,16,64]{2,1,0:T(8,128)(2,1)S(1)} %shard_map.118) | data formatting | bytes 4096

commit v5 on v4

--- a/solution.py
+++ b/solution.py
@@ -374,46 +374,49 @@
     down_load.wait()
     low_lane = iota((CAP // 2, LANES), 1) < LANES // 2
 
-    def down(plane):
+    def down(plane, first_x, size):
+        start = plane * chunk_blocks + first_x * 2
         product = gates * jnp.dot(
             packed,
-            down_buf[:, plane * chunk : (plane + 1) * chunk],
+            down_buf[:, start * LANES : (start + 2 * size) * LANES],
             preferred_element_type=jnp.float32,
         )
-        for j in range(chunk_blocks):
+        for j in range(2 * size):
             block = product[:, j * LANES : (j + 1) * LANES]
             turned = pltpu.roll(block, LANES // 2, 1)
-            owner = plane * PLANE + j * 2
+            owner = (start + j) * 2
             for batch in range(2):
                 low = slice(batch * CAP, batch * CAP + CAP // 2)
                 high = slice(batch * CAP + CAP // 2, (batch + 1) * CAP)
                 comb_out[owner, batch] = jnp.where(low_lane, block[low], turned[high])
                 comb_out[owner + 1, batch] = jnp.where(low_lane, turned[low], block[high])
 
-    def combine(plane):
-        for dx, dy in PLANE_STEPS:
-            target = plane * PLANE + xs[dx] * SIDE + ys[dy]
-            dst = comb_in.at[s, d]
-            for group in (1 - s, s):
-                src = comb_out.at[target, group]
-
-                def send_rows(src=src, dst=dst, group=group, target=target):
-                    pltpu.make_async_remote_copy(
-                        src, dst, comb_send, comb_recv, device_id=(group, target), device_id_type=MESH
-                    ).start()
-
-                if (dx, dy) == (0, 0) and group is s:
-                    pl.when(z != plane)(send_rows)
-
-                    @pl.when(z == plane)
-                    def _(src=src, dst=dst):
-                        pltpu.make_async_copy(src, dst, comb_recv).start()
-                else:
-                    send_rows()
-
-    for plane in (0, 1, 3, 2):
-        down(plane)
-        combine(plane)
+    def combine(plane, first_x, size):
+        for target_x in range(first_x, first_x + size):
+            for dy in (2, 1, 3, 0):
+                target = (plane * SIDE + target_x) * SIDE + ys[dy]
+                dst = comb_in.at[s, d]
+                for group in (1 - s, s):
+                    src = comb_out.at[target, group]
+
+                    def send_rows(src=src, dst=dst, group=group, target=target):
+                        pltpu.make_async_remote_copy(
+                            src, dst, comb_send, comb_recv, device_id=(group, target), device_id_type=MESH
+                        ).start()
+
+                    if dy == 0 and group is s:
+                        pl.when(target != d)(send_rows)
+
+                        @pl.when(target == d)
+                        def _(src=src, dst=dst):
+                            pltpu.make_async_copy(src, dst, comb_recv).start()
+                    else:
+                        send_rows()
+
+    parts = [(0, 0, 1), (0, 1, 1), (0, 2, 2)] + [(plane, 0, 4) for plane in (1, 3, 2)]
+    for part in parts:
+        down(*part)
+        combine(*part)
 
     pltpu.make_async_copy(comb_in, comb_in, comb_recv).wait()
     expert_rows = (comb_in[0] + comb_in[1]).reshape(slots, LANES)

time: 35.6 us -> 35.3 us (level)
  no operation moved by 1% of the time
where the time goes in v5:
time: 35.3 us; the launch traced here: 35.2 us
  Pallas kernels  34.6 us (98%)
  local copies, waits for them, and re-layouts  0.6 us (2%)
    pallas_call x1, Pallas kernels, body(): pl.pallas_call(layer_kernel, out_shape=jax.ShapeDtypeStruct((1, seqs, wid...  34.6 us

profile of v5, /device:TPU:1, one launch (start us, length us, event | category | flops | bytes accessed | tf_op | source)
XLA Modules:
  0.0 35.2 jit_solution(216404579491466237)
XLA Ops:
  0.0 34.6 %shard_map.118 = bf16[1,16,64]{2,1,0:T(8,128)(2,1)S(1)} custom-call(bf16[1,16,4096]{2,1,0:T(8,128)(2,1)} %hidden_hbm.1, bf16[1,1,16,128]{3,2,1,0:T(8,128)(2,1)} %query_hbm.1, bf16[1,1,4096,128]{3,2,1,0:T(8,128)(2,1)} %key_hbm.1, bf16[1,1,4096,128]{3,2,1,0:T(8,128)(2,1)} %value_hbm.1, s32[1,16]{1,0:T(1,128)} %length_hbm.1, s32[2,8,16]{2,1,0:T(8,128)} %bitcast.4, ...), custom_call_target="tpu_custom_call" | custom-call | tf_op jit(solution)/shard_map/pallas_call | solution.py:489
  34.6 0.6 %copy.14 = bf16[1,16,64]{2,1,0:T(8,128)(2,1)} copy(bf16[1,16,64]{2,1,0:T(8,128)(2,1)S(1)} %shard_map.118) | data formatting | bytes 4096

commit v6 on v5

--- a/solution.py
+++ b/solution.py
@@ -12,7 +12,7 @@
 CAP = 4
 SIDE = 4
 PLANE = SIDE * SIDE
-BATCH = 4
+BATCH = 2
 
 
 def hops(step):
@@ -26,6 +26,10 @@
 PLANE_STEPS = far_first([(dx, dy) for dx in range(SIDE) for dy in range(SIDE)])
 CUBE_STEPS = far_first(
     [(dz, dx, dy) for dz in range(SIDE) for dx in range(SIDE) for dy in range(SIDE)]
+)
+
+SUM_STEPS = sorted(
+    CUBE_STEPS, key=lambda p: (-sum(map(hops, p)), (p[0] * 7 + p[1] * 3 + p[2] * 5) % 11)
 )
 
 NEAR_STEPS = [
@@ -267,7 +271,7 @@
         place = block_z[dy % 2][dz] * SIDE + block_x[dy % 2][dx]
         return place * 2 + ys[dy] // 2
 
-    for step in CUBE_STEPS:
+    for step in SUM_STEPS:
         target = at(*step)
         src = part_out.at[block_at(*step)]
         dst = part_in.at[d]
@@ -393,8 +397,9 @@
 
     def combine(plane, first_x, size):
         for target_x in range(first_x, first_x + size):
-            for dy in (2, 1, 3, 0):
-                target = (plane * SIDE + target_x) * SIDE + ys[dy]
+            nearest = plane == 0
+            for dy in (0, 1, 3, 2) if nearest else (2, 1, 3, 0):
+                target = (plane * SIDE + target_x) * SIDE + (dy if nearest else ys[dy])
                 dst = comb_in.at[s, d]
                 for group in (1 - s, s):
                     src = comb_out.at[target, group]
@@ -404,7 +409,7 @@
                             src, dst, comb_send, comb_recv, device_id=(group, target), device_id_type=MESH
                         ).start()
 
-                    if dy == 0 and group is s:
+                    if (nearest or dy == 0) and group is s:
                         pl.when(target != d)(send_rows)
 
                         @pl.when(target == d)
@@ -420,12 +425,9 @@
 
     pltpu.make_async_copy(comb_in, comb_in, comb_recv).wait()
     expert_rows = (comb_in[0] + comb_in[1]).reshape(slots, LANES)
-    routed = jnp.dot(
-        scatter_rows,
-        expert_rows,
-        precision=lax.Precision.HIGHEST,
-        preferred_element_type=jnp.float32,
-    )
+    high_rows = expert_rows.astype(jnp.bfloat16)
+    low_rows = expert_rows - high_rows.astype(jnp.float32)
+    routed = exact_dot(scatter_rows, high_rows) + exact_dot(scatter_rows, low_rows)
     features = out_ref.shape[2]
     pl.when(odd == 1)(res_copy.wait_recv)
     residual = res_in[...]

time: 35.3 us -> 35.3 us (level)
  no operation moved by 1% of the time
where the time goes in v6:
time: 35.3 us; the launch traced here: 35.2 us
  Pallas kernels  34.6 us (98%)
  local copies, waits for them, and re-layouts  0.6 us (2%)
    pallas_call x1, Pallas kernels, body(): pl.pallas_call(layer_kernel, out_shape=jax.ShapeDtypeStruct((1, seqs, wid...  34.6 us

profile of v6, /device:TPU:1, one launch (start us, length us, event | category | flops | bytes accessed | tf_op | source)
XLA Modules:
  0.0 35.2 jit_solution(6052008430816305592)
XLA Ops:
  0.0 34.6 %shard_map.118 = bf16[1,16,64]{2,1,0:T(8,128)(2,1)S(1)} custom-call(bf16[1,16,4096]{2,1,0:T(8,128)(2,1)} %hidden_hbm.1, bf16[1,1,16,128]{3,2,1,0:T(8,128)(2,1)} %query_hbm.1, bf16[1,1,4096,128]{3,2,1,0:T(8,128)(2,1)} %key_hbm.1, bf16[1,1,4096,128]{3,2,1,0:T(8,128)(2,1)} %value_hbm.1, s32[1,16]{1,0:T(1,128)} %length_hbm.1, s32[2,8,16]{2,1,0:T(8,128)} %bitcast.4, ...), custom_call_target="tpu_custom_call" | custom-call | tf_op jit(solution)/shard_map/pallas_call | solution.py:491
  34.6 0.6 %copy.14 = bf16[1,16,64]{2,1,0:T(8,128)(2,1)} copy(bf16[1,16,64]{2,1,0:T(8,128)(2,1)S(1)} %shard_map.118) | data formatting | bytes 4096
